TPU v7x, 32 devices: a whole 2x2x4 slice. The times are simulated.
32 devices in a mesh: row: 4 (over y, x), col: 8 (over z, core).
Axes of the slice: x: 2, y: 2, z: 4, core: 2. Of those that a mesh axis runs over, the one named last changes fastest.
Arguments:
- measurement_tiling_settings: bfloat16 [16384, 40], P(('row', 'col')), may hold values from -4.875 to 4.875
- dest: int32 [16384], P(('row', 'col')), may hold values from 0 to 16383, as said below
- column_tiling_settings: bfloat16 [8192, 40], P('col'), may hold values from -4.875 to 4.875
- entry_layer_weight: bfloat16 [40, 2048], replicated, may hold values from -1 to 1
- entry_layer_bias: float32 [2048], replicated, may hold values from -3 to 3
- middle_layer_weight: bfloat16 [2048, 2048], replicated, may hold values from -0.1875 to 0.1875
- middle_layer_bias: float32 [2048], replicated, may hold values from -3 to 3
- output_layer_weight: bfloat16 [2048, 256], replicated, may hold values from -0.1875 to 0.1875
- relevance_weight_vector: float32 [256], replicated, may hold values from 0.015625 to 0.03125
- probes: float32 [8192, 64], P('col'), may hold values from -2.6516504 to 2.6516504
Outputs:
- product: float32 [16384, 64], P(('row', 'col'))
Inputs may be any that keep to these rules, and one draw needn't show every extreme that they name: dest is a permutation of 0 to 16383, and the measurements held by one device go in equal numbers to the row positions of every device, 16 to each.
All inputs are finite; a program needn't handle non-finite values.
Results may differ from a plain program's by a relative error of at most 0.0088.
Values may be sent and summed in bfloat16 or wider, within the bound.
A program may use at most 64 MiB of HBM per device.

v0:
```python
import jax
import jax.numpy as jnp
from jax import lax
from jax.sharding import PartitionSpec as P


def feature_extractor(inputs, network_weight_list):
    (
        entry_layer_weight,
        entry_layer_bias,
        middle_layer_weight,
        middle_layer_bias,
        output_layer_weight,
    ) = network_weight_list
    hidden = jnp.maximum(
        jnp.dot(inputs, entry_layer_weight, preferred_element_type=jnp.float32) + entry_layer_bias,
        0.0,
    ).astype(jnp.bfloat16)
    hidden = jnp.maximum(
        jnp.dot(hidden, middle_layer_weight, preferred_element_type=jnp.float32)
        + middle_layer_bias,
        0.0,
    ).astype(jnp.bfloat16)
    return jnp.dot(hidden, output_layer_weight, preferred_element_type=jnp.float32).astype(
        jnp.bfloat16
    )


def per_device(
    measurement_tiling_settings,
    dest,
    column_tiling_settings,
    entry_layer_weight,
    entry_layer_bias,
    middle_layer_weight,
    middle_layer_bias,
    output_layer_weight,
    relevance_weight_vector,
    probes,
):
    network_weight_list = (
        entry_layer_weight,
        entry_layer_bias,
        middle_layer_weight,
        middle_layer_bias,
        output_layer_weight,
    )
    sorting_permutation = jnp.argsort(dest)
    sent_ids = dest[sorting_permutation]
    moved, got_ids = (
        lax.all_to_all(
            measurement_tiling_settings[sorting_permutation],
            ("row", "col"),
            split_axis=0,
            concat_axis=0,
            tiled=True,
        ),
        lax.all_to_all(sent_ids, ("row", "col"), split_axis=0, concat_axis=0, tiled=True),
    )
    got_feats = feature_extractor(moved, network_weight_list)
    placed = got_feats[jnp.argsort(got_ids)]
    row_feature_matrix = lax.all_gather(placed, "col", axis=0, tiled=True)
    row_total = row_feature_matrix.shape[0]
    block_rows = min(512, row_total)
    blocks = row_total // block_rows
    row_float = row_feature_matrix.astype(jnp.float32)
    scaled = (
        (row_float * relevance_weight_vector)
        .astype(jnp.bfloat16)
        .reshape(blocks, block_rows, row_feature_matrix.shape[1])
    )
    sq_row = jnp.sum(relevance_weight_vector * jnp.square(row_float), axis=1).reshape(
        blocks, block_rows
    )
    col_share = column_tiling_settings.shape[0] // lax.axis_size("row")
    own_cols = lax.dynamic_slice_in_dim(
        column_tiling_settings, lax.axis_index("row") * col_share, col_share, 0
    )
    col_feats = feature_extractor(own_cols, network_weight_list)
    empty = jnp.zeros((row_total, probes.shape[1]), jnp.float32)
    piece = lax.all_gather(col_feats, "row", axis=0, tiled=True)
    sq_col = jnp.sum(relevance_weight_vector * jnp.square(piece.astype(jnp.float32)), axis=1)

    def one_block(pieces):
        scaled_rows, sq_rows = pieces
        cross = lax.dot_general(
            scaled_rows, piece, (((1,), (1,)), ((), ())), preferred_element_type=jnp.float32
        )
        kern = jnp.exp(-0.5 * (sq_rows[:, None] + sq_col[None, :] - 2.0 * cross))
        return jnp.dot(
            kern, probes, precision=lax.Precision.HIGHEST, preferred_element_type=jnp.float32
        )

    added = lax.map(one_block, (scaled, sq_row))
    partial_sums = added.reshape(empty.shape)
    return lax.psum_scatter(partial_sums, "col", scatter_dimension=0, tiled=True)


def solution(mesh):
    placed = (
        P(("row", "col"), None),
        P(("row", "col")),
        P("col", None),
        P(),
        P(),
        P(),
        P(),
        P(),
        P(),
        P("col", None),
    )
    return jax.shard_map(
        per_device, mesh=mesh, in_specs=placed, out_specs=P(("row", "col"), None), check_vma=False
    )
```

profile of v0, /device:TPU:0, one launch (start us, length us, event | category | flops | bytes accessed | tf_op | source)
XLA Modules:
  0.0 169.2 jit_solution(2201544675280311176)
XLA Ops:
  6.6 4.5 %sort.31 = (s32[512]{0:T(512)}, s32[512]{0:T(512)S(1)}) sort(s32[512]{0:T(512)} %param.13, s32[512]{0:T(512)S(1)} %iota.7), dimensions={0}, to_apply=%region_0.0 | sort | flops 4608 | bytes 8192 | tf_op jit(solution)/shard_map/jit(argsort)/sort | solution.py:48
  11.1 3.6 %gather_fusion.1 = s32[512]{0:T(512)S(1)} fusion(s32[512]{0:T(512)} %param.13, s32[1024]{0:T(1024)S(1)} %pad_clamp_fusion.1), kind=kCustom, calls=%fused_computation.1 | custom fusion | bytes 6144 | tf_op jit(solution)/shard_map/gather | solution.py:49
  14.7 0.7 all_to_all.19
  15.4 7.3 %all-to-all-start.1 = ((s32[32,16,1]{1,2,0:T(1,128)}), s32[32,16,1]{1,2,0:T(1,128)S(1)}, u32[]{:S(2)}, u32[]{:S(2)}) async-start(s32[32,16,1]{1,2,0:T(1,128)} %bitcast.5), calls=%async_computation.1 | async-start | bytes 32768 | tf_op jit(solution)/shard_map/all_to_all | solution.py:58
  22.9 1.3 gather_fusion
  24.2 0.8 reshape.59
  25.0 4.8 %all-to-all-done.1 = s32[32,16,1]{1,2,0:T(1,128)S(1)} async-done(((s32[32,16,1]{1,2,0:T(1,128)}), s32[32,16,1]{1,2,0:T(1,128)S(1)}, u32[]{:S(2)}, u32[]{:S(2)}) %all-to-all-start.1) | async-done | bytes 2080 | tf_op jit(solution)/shard_map/all_to_all | solution.py:58
  29.9 2.6 %all-to-all-start = ((bf16[32,2,320]{2,1,0:T(2,128)(2,1)}), bf16[32,2,320]{2,1,0:T(2,128)(2,1)S(1)}, u32[]{:S(2)}, u32[]{:S(2)}) async-start(bf16[32,2,320]{2,1,0:T(2,128)(2,1)} %reshape.59), calls=%async_computation | async-start | bytes 98304 | tf_op jit(solution)/shard_map/all_to_all | solution.py:51
  32.5 0.6 broadcast.59
  33.1 0.7 reduce.3
  33.9 3.8 %sort.32 = (s32[512]{0:T(512)}, s32[512]{0:T(512)S(1)}) sort(s32[512]{0:T(512)S(1)} %all_to_all.21, s32[512]{0:T(512)S(1)} %iota.8), dimensions={0}, to_apply=%region_1.2 | sort | flops 4608 | bytes 8192 | tf_op jit(solution)/shard_map/jit(argsort)/sort | solution.py:61
  37.7 2.0 %all-to-all-done = bf16[32,2,320]{2,1,0:T(2,128)(2,1)S(1)} async-done(((bf16[32,2,320]{2,1,0:T(2,128)(2,1)}), bf16[32,2,320]{2,1,0:T(2,128)(2,1)S(1)}, u32[]{:S(2)}, u32[]{:S(2)}) %all-to-all-start) | async-done | bytes 40992 | tf_op jit(solution)/shard_map/all_to_all | solution.py:51
  39.9 8.9 %maximum_convert_fusion = bf16[512,2048]{1,0:T(8,128)(2,1)} fusion(bf16[2048,2048]{1,0:T(8,128)(2,1)} %param.17, f32[2048]{0:T(1024)S(1)} %copy-done.5, bf16[512,40]{1,0:T(8,128)(2,1)S(1)} %bitcast.40, bf16[40,2048]{1,0:T(8,128)(2,1)S(1)} %copy-done.4, f32[2048]{0:T(1024)S(1)} %copy-done.6), kind=kOutput, calls=%fused_computation.26 | convolution fusion | flops 4385144832 | bytes 10706944 | tf_op jit(solution)/shard_map/dot_general | solution.py:20
  48.9 2.3 %convolution_convert_fusion = bf16[512,256]{1,0:T(8,128)(2,1)S(1)} fusion(bf16[512,2048]{1,0:T(8,128)(2,1)} %maximum_convert_fusion, bf16[2048,256]{1,0:T(8,128)(2,1)S(1)} %copy-done), kind=kOutput, calls=%fused_computation.34 | convolution fusion | flops 537001984 | bytes 3407872 | tf_op jit(solution)/shard_map/dot_general | solution.py:24
  51.2 2.6 %gather_fusion.2 = bf16[512,256]{1,0:T(8,128)(2,1)} fusion(bf16[512,256]{1,0:T(8,128)(2,1)S(1)} %convolution_convert_fusion, s32[1024]{0:T(1024)S(1)} %pad_clamp_fusion), kind=kCustom, calls=%fused_computation.2 | custom fusion | bytes 526336 | tf_op jit(solution)/shard_map/gather | solution.py:61
  53.8 6.0 %fusion.25 = bf16[256,2048]{1,0:T(8,128)(2,1)S(1)} fusion(bf16[2048,2048]{1,0:T(8,128)(2,1)} %param.17, bf16[40,2048]{1,0:T(8,128)(2,1)S(1)} %copy-done.4, f32[2048]{0:T(1024)S(1)} %copy-done.5, f32[2048]{0:T(1024)S(1)} %copy-done.6, bf16[1024,40]{0,1:T(8,128)(2,1)} %param.14, s32[]{:T(128)S(6)} %select_n.12), kind=kOutput, calls=%fused_computation.33 | convolution fusion | flops 2192572416 | bytes 9637892 | tf_op jit(solution)/shard_map/dot_general | solution.py:20
  59.9 0.4 convolution_convert_fusion.1
  60.3 9.4 %all_gather.7 = bf16[1024,256]{1,0:T(8,128)(2,1)S(1)} all-gather(bf16[256,256]{1,0:T(8,128)(2,1)S(1)} %convolution_convert_fusion.1), channel_id=1, replica_groups=mesh['row'=4,'col'=8] {'row'}, dimensions={0}, use_global_device_ids=true | all-gather | bytes 655360 | tf_op jit(solution)/shard_map/all_gather | solution.py:81
  69.7 0.2 multiply_reduce_fusion
  70.0 12.3 %all-gather.3.cloned.1.call-done = bf16[4096,256]{1,0:T(8,128)(2,1)} async-done(((bf16[512,256]{1,0:T(8,128)(2,1)}), bf16[4096,256]{1,0:T(8,128)(2,1)}) %all-gather.3.cloned.1.call-update) | async-done | bytes 2097168 | tf_op jit(solution)/shard_map/all_gather | solution.py:62
  82.2 3.7 %fusion.21 = (bf16[4096,256]{1,0:T(8,128)(2,1)}, f32[4096]{0:T(1024)S(1)}) fusion(bf16[4096,256]{1,0:T(8,128)(2,1)} %all-gather.3.cloned.1.call-done, f32[256]{0:T(256)S(1)} %copy-done.2), kind=kLoop, calls=%fused_computation.25 | loop fusion | flops 6287360 | bytes 4211712 | tf_op jit(solution)/shard_map/convert_element_type | solution.py:69
  85.9 43.0 %while.10 = (s32[]{:T(128)}, f32[8,512,64]{1,0,2:T(8,128)S(1)}, f32[8,512]{1,0:T(8,128)S(1)}, f32[1024]{0:T(1024)S(1)}, bf16[8,512,256]{2,1,0:T(8,128)(2,1)}, /*...) while((s32[]{:T(128)}, f32[8,512,64]{1,0,2:T(8,128)S(1)}, ...), condition=%wide.region_5.6_spmd, body=%wide.region_4.5_spmd.sunk | while | flops 673185792 | bytes 5909093 | solution.py:94
  85.9 1.4 fusion.55
  87.4 2.6 %fusion.56 = f32[1,512,64]{1,2,0:T(8,128)S(1)} fusion(f32[1024,64]{0,1:T(8,128)S(1)} %get-tuple-element.130, f32[512,1024]{1,0:T(8,128)S(1)} %fusion.55, f32[1024]{0:T(1024)S(1)} %get-tuple-element.127, f32[512]{0:T(512)S(1)} %bitcast.41), kind=kOutput, calls=%fused_computation.9.clone.1 | convolution fusion | flops 404750336 | bytes 2496512 | tf_op jit(solution)/shard_map/while/body/eval_jaxpr/dot_general | solution.py:90
  90.2 1.1 dynamic_update_slice.5
  91.3 1.4 fusion.55
  92.8 2.6 %fusion.56 = f32[1,512,64]{1,2,0:T(8,128)S(1)} fusion(f32[1024,64]{0,1:T(8,128)S(1)} %get-tuple-element.130, f32[512,1024]{1,0:T(8,128)S(1)} %fusion.55, f32[1024]{0:T(1024)S(1)} %get-tuple-element.127, f32[512]{0:T(512)S(1)} %bitcast.41), kind=kOutput, calls=%fused_computation.9.clone.1 | convolution fusion | flops 404750336 | bytes 2496512 | tf_op jit(solution)/shard_map/while/body/eval_jaxpr/dot_general | solution.py:90
  95.5 1.1 dynamic_update_slice.5
  96.7 1.4 fusion.55
  98.1 2.6 %fusion.56 = f32[1,512,64]{1,2,0:T(8,128)S(1)} fusion(f32[1024,64]{0,1:T(8,128)S(1)} %get-tuple-element.130, f32[512,1024]{1,0:T(8,128)S(1)} %fusion.55, f32[1024]{0:T(1024)S(1)} %get-tuple-element.127, f32[512]{0:T(512)S(1)} %bitcast.41), kind=kOutput, calls=%fused_computation.9.clone.1 | convolution fusion | flops 404750336 | bytes 2496512 | tf_op jit(solution)/shard_map/while/body/eval_jaxpr/dot_general | solution.py:90
  100.9 1.1 dynamic_update_slice.5
  102.1 1.4 fusion.55
  103.5 2.6 %fusion.56 = f32[1,512,64]{1,2,0:T(8,128)S(1)} fusion(f32[1024,64]{0,1:T(8,128)S(1)} %get-tuple-element.130, f32[512,1024]{1,0:T(8,128)S(1)} %fusion.55, f32[1024]{0:T(1024)S(1)} %get-tuple-element.127, f32[512]{0:T(512)S(1)} %bitcast.41), kind=kOutput, calls=%fused_computation.9.clone.1 | convolution fusion | flops 404750336 | bytes 2496512 | tf_op jit(solution)/shard_map/while/body/eval_jaxpr/dot_general | solution.py:90
  106.3 1.1 dynamic_update_slice.5
  107.4 1.4 fusion.55
  108.9 2.6 %fusion.56 = f32[1,512,64]{1,2,0:T(8,128)S(1)} fusion(f32[1024,64]{0,1:T(8,128)S(1)} %get-tuple-element.130, f32[512,1024]{1,0:T(8,128)S(1)} %fusion.55, f32[1024]{0:T(1024)S(1)} %get-tuple-element.127, f32[512]{0:T(512)S(1)} %bitcast.41), kind=kOutput, calls=%fused_computation.9.clone.1 | convolution fusion | flops 404750336 | bytes 2496512 | tf_op jit(solution)/shard_map/while/body/eval_jaxpr/dot_general | solution.py:90
  111.7 1.1 dynamic_update_slice.5
  112.8 1.4 fusion.55
  114.3 2.6 %fusion.56 = f32[1,512,64]{1,2,0:T(8,128)S(1)} fusion(f32[1024,64]{0,1:T(8,128)S(1)} %get-tuple-element.130, f32[512,1024]{1,0:T(8,128)S(1)} %fusion.55, f32[1024]{0:T(1024)S(1)} %get-tuple-element.127, f32[512]{0:T(512)S(1)} %bitcast.41), kind=kOutput, calls=%fused_computation.9.clone.1 | convolution fusion | flops 404750336 | bytes 2496512 | tf_op jit(solution)/shard_map/while/body/eval_jaxpr/dot_general | solution.py:90
  117.0 1.1 dynamic_update_slice.5
  118.2 1.4 fusion.55
  119.6 2.6 %fusion.56 = f32[1,512,64]{1,2,0:T(8,128)S(1)} fusion(f32[1024,64]{0,1:T(8,128)S(1)} %get-tuple-element.130, f32[512,1024]{1,0:T(8,128)S(1)} %fusion.55, f32[1024]{0:T(1024)S(1)} %get-tuple-element.127, f32[512]{0:T(512)S(1)} %bitcast.41), kind=kOutput, calls=%fused_computation.9.clone.1 | convolution fusion | flops 404750336 | bytes 2496512 | tf_op jit(solution)/shard_map/while/body/eval_jaxpr/dot_general | solution.py:90
  122.4 1.1 dynamic_update_slice.5
  123.6 1.4 fusion.55
  125.0 2.6 %fusion.56 = f32[1,512,64]{1,2,0:T(8,128)S(1)} fusion(f32[1024,64]{0,1:T(8,128)S(1)} %get-tuple-element.130, f32[512,1024]{1,0:T(8,128)S(1)} %fusion.55, f32[1024]{0:T(1024)S(1)} %get-tuple-element.127, f32[512]{0:T(512)S(1)} %bitcast.41), kind=kOutput, calls=%fused_computation.9.clone.1 | convolution fusion | flops 404750336 | bytes 2496512 | tf_op jit(solution)/shard_map/while/body/eval_jaxpr/dot_general | solution.py:90
  127.8 1.1 dynamic_update_slice.5
  128.9 1.6 copy.22
  130.6 31.8 %reduce-scatter.2.cloned.1.call-done = f32[512,64]{0,1:T(8,128)} async-done(((f32[4096,64]{0,1:T(8,128)}), f32[512,64]{0,1:T(8,128)}) %reduce-scatter.2.cloned.1.call-update) | async-done | bytes 131088 | tf_op jit(solution)/shard_map/reduce_scatter | solution.py:96
  (45 shorter events, 1.7 us)
Async XLA Ops:
  6.5 42.3 %copy-start = (bf16[2048,256]{1,0:T(8,128)(2,1)S(1)}, bf16[2048,256]{1,0:T(8,128)(2,1)}, u32[]{:S(2)}) copy-start(bf16[2048,256]{1,0:T(8,128)(2,1)} %param.19) | copy-start | bytes 3145732
  6.5 16.2 %copy-start.1 = (bf16[512,40]{0,1:T(8,128)(2,1)S(1)}, bf16[512,40]{0,1:T(8,128)(2,1)}, u32[]{:S(2)}) copy-start(bf16[512,40]{0,1:T(8,128)(2,1)} %param.12) | copy-start | bytes 122884
  6.5 33.4 %copy-start.4 = (bf16[40,2048]{1,0:T(8,128)(2,1)S(1)}, bf16[40,2048]{1,0:T(8,128)(2,1)}, u32[]{:S(2)}) copy-start(bf16[40,2048]{1,0:T(8,128)(2,1)} %param.15) | copy-start | bytes 491524
  6.5 33.4 %copy-start.6 = (f32[2048]{0:T(1024)S(1)}, f32[2048]{0:T(1024)}, u32[]{:S(2)}) copy-start(f32[2048]{0:T(1024)} %param.16) | copy-start | bytes 24580
  6.5 33.4 %copy-start.5 = (f32[2048]{0:T(1024)S(1)}, f32[2048]{0:T(1024)}, u32[]{:S(2)}) copy-start(f32[2048]{0:T(1024)} %param.18) | copy-start | bytes 24580
  15.4 14.4 %all-to-all-start.1 = ((s32[32,16,1]{1,2,0:T(1,128)}), s32[32,16,1]{1,2,0:T(1,128)S(1)}, u32[]{:S(2)}, u32[]{:S(2)}) async-start(s32[32,16,1]{1,2,0:T(1,128)} %bitcast.5), calls=%async_computation.1 | async-start | bytes 32768 | tf_op jit(solution)/shard_map/all_to_all | solution.py:58
  29.9 9.9 %all-to-all-start = ((bf16[32,2,320]{2,1,0:T(2,128)(2,1)}), bf16[32,2,320]{2,1,0:T(2,128)(2,1)S(1)}, u32[]{:S(2)}, u32[]{:S(2)}) async-start(bf16[32,2,320]{2,1,0:T(2,128)(2,1)} %reshape.59), calls=%async_computation | async-start | bytes 98304 | tf_op jit(solution)/shard_map/all_to_all | solution.py:51
  32.4 49.8 %all-gather.3.cloned.1.call-start = ((), (), s32[]{:S(2)}) async-start(), calls=%async_computation.4 | async-start | bytes 2359296 | tf_op jit(solution)/shard_map/all_gather | solution.py:62
  53.8 108.6 %reduce-scatter.2.cloned.1.call-start = ((), (), s32[]{:S(2)}) async-start(), calls=%async_computation.3 | async-start | bytes 1179648 | tf_op jit(solution)/shard_map/reduce_scatter | solution.py:96
  59.9 9.8 %copy-start.2 = (f32[256]{0:T(256)S(1)}, f32[256]{0:T(256)}, u32[]{:S(2)}) copy-start(f32[256]{0:T(256)} %param.20) | copy-start | bytes 3076
  69.9 16.0 %copy-start.3 = (f32[1024,64]{0,1:T(8,128)S(1)}, f32[1024,64]{0,1:T(8,128)}, u32[]{:S(2)}) copy-start(f32[1024,64]{0,1:T(8,128)} %param.21) | copy-start | bytes 786436
Sparse Core Ops, SparseCore 0:
  53.9 28.2 all-gather.2
  130.7 31.6 reduce-scatter.1
where the time goes:
time: 170 us; the launch traced here: 169 us
  waiting for transfers between devices  51 us (30%)
  matrix products  50.2 us (30%)
  local copies, waits for them, and re-layouts  21.8 us (13%)
  between operations  13.6 us (8%)
  other arithmetic  13 us (8%)
  starting transfers between devices  9.95 us (6%)
  blocking collectives  9.38 us (6%)
    reduce_scatter x1, waiting for transfers between devices, per_device(): lax.psum_scatter(partial_sums, 'col', scatter_dimension=0, tiled=True)  31.8 us
    dot_general x8, matrix products, one_block(): jnp.dot(kern, probes, precision=lax.Precision.HIGHEST, preferred_element_...  21.1 us
    dot_general x2, matrix products, feature_extractor(): jnp.dot(hidden, middle_layer_weight, preferred_element_type=jnp.float32)  15 us
    all_gather x1, waiting for transfers between devices, per_device(): row_feature_matrix = lax.all_gather(placed, 'col', axis=0, tiled=True)  12.3 us
    dot_general x8, matrix products, one_block(): lax.dot_general(scaled_rows, piece, (((1,), (1,)), ((), ())), preferred_e...  11.4 us
    dynamic_update_slice x16, local copies, waits for them, and re-layouts, per_device(): added = lax.map(one_block, (scaled, sq_row))  10.1 us
    all_gather x1, blocking collectives, per_device(): piece = lax.all_gather(col_feats, 'row', axis=0, tiled=True)  9.38 us
    all_to_all x1, starting transfers between devices, per_device(): lax.all_to_all(sent_ids, ('row', 'col'), split_axis=0, concat_axis=0, til...  7.3 us
  transfers between devices with their start and end apart: 4, of which 4 were waited for; matrix products, arithmetic and copies ran while one was open for 8% of the time, Pallas kernels for 0%

commit v1 on v0

v1 whole, which is shorter than its diff:
```python
import functools

import jax
import jax.numpy as jnp
from jax import lax
from jax.experimental import pallas as pl
from jax.experimental.pallas import tpu as pltpu
from jax.sharding import PartitionSpec as P

BF = jnp.bfloat16
F32 = jnp.float32
NN = (((1,), (0,)), ((), ()))
NT = (((1,), (1,)), ((), ()))
TN = (((0,), (0,)), ((), ()))
MESH = pl.DeviceIdType.MESH
CHUNKS = 4


def mm(a, b, dims=NN):
    return lax.dot_general(a, b, dims, preferred_element_type=F32)


def kernel(
    n_row, n_col, slot,
    x_ref, dest_ref, cx_ref, w1_ref, b1_ref, w2_hbm, b2_ref, w3_hbm, rel_ref, probes_ref,
    out_ref,
    w2, w3, h1, h2, sent, got, colg, rowf, scaled, half_row, acc, part, parts_in,
    w_sem, a_send, a_recv, c_send, c_recv, f_send, r_send, r_recv, p_send, p_recv,
):
    n_dev = n_row * n_col
    rows, width = x_ref.shape
    hid = w1_ref.shape[1]
    feat = w3.shape[1]
    npr = probes_ref.shape[1]
    cols = cx_ref.shape[0] // n_row
    step = hid // CHUNKS
    slots = n_dev * slot
    mr, mc = lax.axis_index("row"), lax.axis_index("col")
    me = mr * n_col + mc
    core, chip, n_chip = mc % 2, mc // 2, n_col // 2
    sibling = mc + 1 - 2 * core

    w_copies = [
        pltpu.make_async_copy(w2_hbm.at[:, pl.ds(n * step, step)], w2.at[n], w_sem.at[n])
        for n in range(CHUNKS)
    ]
    w_copies.append(pltpu.make_async_copy(w3_hbm, w3, w_sem.at[CHUNKS]))
    for one in w_copies:
        one.start()

    barrier = pltpu.get_barrier_semaphore()

    @pl.loop(1, n_dev)
    def _(off):
        to = (me + off) % n_dev
        pl.semaphore_signal(
            barrier, inc=1, device_id=(to // n_col, to % n_col), device_id_type=MESH
        )

    bits = rows.bit_length() - 1
    dest = dest_ref[...]
    target = lax.shift_right_logical(dest, jnp.full_like(dest, bits))
    place = lax.bitwise_and(dest, jnp.full_like(dest, rows - 1)) + 1
    one_hot = (lax.broadcasted_iota(jnp.int32, (n_dev, rows), 0) == target).astype(F32)
    before = (
        lax.broadcasted_iota(jnp.int32, (rows, rows), 0)
        < lax.broadcasted_iota(jnp.int32, (rows, rows), 1)
    ).astype(F32).astype(BF)
    count = mm(one_hot.astype(BF), before)
    within = jnp.sum(one_hot * count, axis=0, keepdims=True)
    key = target * slot + within.astype(jnp.int32)
    pick = (lax.broadcasted_iota(jnp.int32, (slots, rows), 0) == key).astype(F32).astype(BF)
    high = lax.shift_right_logical(place, jnp.full_like(place, 5)).astype(F32)
    low = lax.bitwise_and(place, jnp.full_like(place, 31)).astype(F32)
    line = lax.broadcasted_iota(jnp.int32, (128, rows), 0)
    marks = jnp.where(line == width, high, jnp.where(line == width + 1, low, 0.0)).astype(BF)
    sent[...] = mm(pick, marks, NT).astype(BF).reshape(n_dev, slot, 128)
    sent[:, :, :width] = mm(pick, x_ref[...]).astype(BF).reshape(n_dev, slot, width)
    got[me] = sent[me]

    pl.semaphore_wait(barrier, n_dev - 1)

    def a2a(to, sem_at):
        return pltpu.make_async_remote_copy(
            src_ref=sent.at[to], dst_ref=got.at[sem_at],
            send_sem=a_send.at[to], recv_sem=a_recv.at[sem_at],
            device_id=(to // n_col, to % n_col), device_id_type=MESH,
        )

    @pl.loop(1, n_dev)
    def _(off):
        a2a((me + off) % n_dev, me).start()

    def layers(x, m, first, between=None):
        for n in range(CHUNKS):
            at = pl.ds(n * step, step)
            h1[:m, at] = jnp.maximum(mm(x, w1_ref[:, at]) + b1_ref[:, at], 0.0).astype(BF)
        if first:
            for one in w_copies[:CHUNKS]:
                one.wait()

        @pl.loop(0, CHUNKS)
        def _(n):
            at = pl.ds(pl.multiple_of(n * step, step), step)
            h2[:m, at] = jnp.maximum(mm(h1[:m, :], w2[n]) + b2_ref[:, at], 0.0).astype(BF)

        if first:
            w_copies[CHUNKS].wait()
        if between is not None:
            between()
        return mm(h2[:m, :], w3[...]).astype(BF)

    mine = pl.ds(pl.multiple_of(mr * cols, cols), cols)
    rel = rel_ref[...]
    cf = layers(cx_ref[mine, :], cols, True)
    colg[mc, :cols, :] = cf
    eye = (
        lax.broadcasted_iota(jnp.int32, (cols, cols), 0)
        == lax.broadcasted_iota(jnp.int32, (cols, cols), 1)
    ).astype(F32).astype(BF)
    colg[mc, pl.ds(cols, npr), :] = mm(probes_ref[mine, :].astype(BF), eye, TN).astype(BF)
    cf32 = cf.astype(F32)
    half_col = lax.dot_general(
        jnp.broadcast_to(0.5 * rel, (16, feat)), cf32 * cf32, NT,
        precision=lax.Precision.HIGHEST, preferred_element_type=F32,
    )
    top = half_col.astype(BF).astype(F32)
    mid = (half_col - top).astype(BF).astype(F32)
    bottom = half_col - top - mid
    row_no = lax.broadcasted_iota(jnp.int32, (16, cols), 0)
    colg[mc, pl.ds(cols + npr, 16), :] = jnp.where(
        row_no == 0, top, jnp.where(row_no == 1, mid, jnp.where(row_no == 2, bottom, 0.0))
    ).astype(BF)

    def col_copy(block, to, send):
        return pltpu.make_async_remote_copy(
            src_ref=colg.at[block], dst_ref=colg.at[block],
            send_sem=send, recv_sem=c_recv.at[block],
            device_id=(mr, to), device_id_type=MESH,
        )

    def mate(k):
        return ((chip + k) % n_chip) * 2 + core

    col_sends = [col_copy(mc, mate(n_chip - k), c_send.at[k]) for k in range(1, n_chip)]
    col_sends.append(col_copy(mc, sibling, c_send.at[0]))
    for one in col_sends:
        one.start()

    @pl.loop(1, n_dev)
    def _(off):
        a2a(me, (me + n_dev - off) % n_dev).wait_recv()

    came = got[...].reshape(slots, 128)
    came32 = came.astype(F32)
    spot = came32[:, width : width + 1] * 32.0 + came32[:, width + 1 : width + 2]
    put = (
        spot.astype(jnp.int32) == lax.broadcasted_iota(jnp.int32, (slots, rows), 1) + 1
    ).astype(F32).astype(BF)
    xp = mm(put, came, TN).astype(BF)

    forwards = [col_copy(mate(k), sibling, f_send.at[k]) for k in range(1, n_chip)]

    def forward():
        for k in range(1, n_chip):
            col_copy(mate(k), sibling, f_send.at[k]).wait_recv()
            forwards[k - 1].start()

    rowf[mr] = layers(xp[:, :width], rows, False, forward)

    def row_copy(block, to, send):
        return pltpu.make_async_remote_copy(
            src_ref=rowf.at[block], dst_ref=rowf.at[block],
            send_sem=send, recv_sem=r_recv.at[block],
            device_id=(to, mc), device_id_type=MESH,
        )

    row_sends = [row_copy(mr, (mr + n_row - k) % n_row, r_send.at[k]) for k in range(1, n_row)]
    for one in row_sends:
        one.start()

    for k in range(n_chip):
        other = ((chip + k) % n_chip) * 2 + 1 - core
        col_copy(other, sibling, f_send.at[0]).wait_recv()

    half = rows // 2
    part_sends = []
    for k in range(n_row):
        block = (mr + k) % n_row
        if k:
            row_copy(block, block, r_send.at[0]).wait_recv()
        rf = rowf[block].astype(F32)
        scaled[...] = (rf * rel).astype(BF)
        half_row[...] = jnp.broadcast_to(
            0.5 * jnp.sum(rel * (rf * rf), axis=1, keepdims=True), half_row.shape
        )
        acc[...] = jnp.zeros_like(acc)

        @pl.loop(0, n_col)
        def _(c):
            cross = mm(scaled[...], colg[c, :cols, :], NT)
            sq = colg[c, pl.ds(cols + npr, 16), :].astype(F32)
            sq_col = sq[0:1, :] + sq[1:2, :] + sq[2:3, :]
            kern = jnp.exp(cross - (half_row[...] + sq_col)).astype(BF)
            acc[...] += mm(kern, colg[c, pl.ds(cols, npr), :], NT)

        if k:
            part[k - 1] = jnp.concatenate([acc[:half, :], acc[half:, :]], axis=1).astype(BF)
            one = pltpu.make_async_remote_copy(
                src_ref=part.at[k - 1], dst_ref=parts_in.at[k - 1],
                send_sem=p_send.at[k - 1], recv_sem=p_recv.at[k - 1],
                device_id=(block, mc), device_id_type=MESH,
            )
            one.start()
            part_sends.append(one)
        else:
            out_ref[...] = acc[...]

    for k in range(n_row - 1):
        part_sends[k].wait_recv()
    total = parts_in[0].astype(F32)
    for k in range(1, n_row - 1):
        total += parts_in[k].astype(F32)
    out_ref[:half, :] += total[:, :npr]
    out_ref[half:, :] += total[:, npr:]

    @pl.loop(1, n_dev)
    def _(off):
        a2a((me + off) % n_dev, me).wait_send()

    for one in col_sends + forwards + row_sends + part_sends:
        one.wait_send()


def per_device(n_row, n_col, x, dest, cx, w1, b1, w2, b2, w3, rel, probes):
    n_dev = n_row * n_col
    rows, feat, hid, npr = x.shape[0], w3.shape[1], w1.shape[1], probes.shape[1]
    cols = cx.shape[0] // n_row
    slot = -(-(rows // n_dev) // 16) * 16
    tall = max(rows, cols)
    vmem = pl.BlockSpec(memory_space=pltpu.VMEM)
    hbm = pl.BlockSpec(memory_space=pl.ANY)
    dma = pltpu.SemaphoreType.DMA
    return pl.pallas_call(
        functools.partial(kernel, n_row, n_col, slot),
        out_shape=jax.ShapeDtypeStruct((rows, npr), F32),
        in_specs=[vmem] * 5 + [hbm, vmem, hbm, vmem, vmem],
        out_specs=vmem,
        scratch_shapes=[
            pltpu.VMEM((CHUNKS, hid, hid // CHUNKS), BF),
            pltpu.VMEM((hid, feat), BF),
            pltpu.VMEM((tall, hid), BF),
            pltpu.VMEM((tall, hid), BF),
            pltpu.VMEM((n_dev, slot, 128), BF),
            pltpu.VMEM((n_dev, slot, 128), BF),
            pltpu.VMEM((n_col, cols + npr + 16, feat), BF),
            pltpu.VMEM((n_row, rows, feat), BF),
            pltpu.VMEM((rows, feat), BF),
            pltpu.VMEM((rows, cols), F32),
            pltpu.VMEM((rows, npr), F32),
            pltpu.VMEM((n_row - 1, rows // 2, 2 * npr), BF),
            pltpu.VMEM((n_row - 1, rows // 2, 2 * npr), BF),
            dma((CHUNKS + 1,)),
            dma((n_dev,)),
            dma((n_dev,)),
            dma((n_col // 2,)),
            dma((n_col,)),
            dma((n_col // 2,)),
            dma((n_row,)),
            dma((n_row,)),
            dma((n_row,)),
            dma((n_row,)),
        ],
        compiler_params=pltpu.CompilerParams(
            collective_id=0, has_side_effects=True, vmem_limit_bytes=48 * 2**20
        ),
    )(x, dest.reshape(1, -1), cx, w1, b1.reshape(1, -1), w2, b2.reshape(1, -1), w3,
      rel.reshape(1, -1), probes)


def solution(mesh):
    placed = (
        P(("row", "col"), None),
        P(("row", "col")),
        P("col", None),
        P(),
        P(),
        P(),
        P(),
        P(),
        P(),
        P("col", None),
    )
    return jax.shard_map(
        functools.partial(per_device, mesh.shape["row"], mesh.shape["col"]),
        mesh=mesh, in_specs=placed, out_specs=P(("row", "col"), None), check_vma=False,
    )
```

time: 170 us -> 62.7 us (0.37)
  Pallas kernels: 0 us -> 53.4 us
  waiting for transfers between devices: 51 us -> 0 us
  matrix products: 50.2 us -> 0 us
  between operations: 13.6 us -> 0.04 us
  local copies, waits for them, and re-layouts: 21.8 us -> 8.77 us
  other arithmetic: 13 us -> 0 us
  starting transfers between devices: 9.95 us -> 0 us
  blocking collectives: 9.38 us -> 0 us
    pallas_call x0 -> x1, Pallas kernels: none -> 53.4 us  [per_device(): pl.pallas_call(functools.partial(kernel, n_row, n_col, slot), out_shape=j...]
    dot_general x20 -> x0, matrix products: 50.2 us -> none  [the longest x8 21.1 us: one_block(): jnp.dot(kern, probes, precision=lax.Precision.HIGHEST, preferred_element_...]
    reduce_scatter x1 -> x0, waiting for transfers between devices: 31.8 us -> none  [per_device(): lax.psum_scatter(partial_sums, 'col', scatter_dimension=0, tiled=True)]
    all_gather x1 -> x0, waiting for transfers between devices: 12.3 us -> none  [per_device(): row_feature_matrix = lax.all_gather(placed, 'col', axis=0, tiled=True)]
    dynamic_update_slice x16 -> x0, local copies, waits for them, and re-layouts: 10.1 us -> none  [per_device(): added = lax.map(one_block, (scaled, sq_row))]
    all_to_all x2 -> x0, starting transfers between devices: 9.87 us -> none  [the longest x1 7.3 us: per_device(): lax.all_to_all(sent_ids, ('row', 'col'), split_axis=0, concat_axis=0, til...]
    all_gather x1 -> x0, blocking collectives: 9.38 us -> none  [per_device(): piece = lax.all_gather(col_feats, 'row', axis=0, tiled=True)]
    sort x2 -> x0, other arithmetic: 8.33 us -> none  [the longest x1 4.54 us: per_device(): sorting_permutation = jnp.argsort(dest)]
  transfers between devices with their start and end apart: 4 -> 0, of which waited for: 4 -> 0; matrix products, arithmetic and copies ran while one was open for 8% -> 0% of each run, Pallas kernels for 0% -> 0%
where the time goes in v1:
time: 62.7 us; the launch traced here: 62.2 us
  Pallas kernels  53.4 us (85%)
  local copies, waits for them, and re-layouts  8.77 us (14%)
    pallas_call x1, Pallas kernels, per_device(): pl.pallas_call(functools.partial(kernel, n_row, n_col, slot), out_shape=j...  53.4 us
    unnamed x15, local copies, waits for them, and re-layouts  7.99 us

profile of v1, /device:TPU:0, one launch (start us, length us, event | category | flops | bytes accessed | tf_op | source)
XLA Modules:
  0.0 62.2 jit_solution(4060387968067822850)
XLA Ops:
  0.0 0.9 %copy.11.x_ref = bf16[512,40]{1,0:T(8,128)(2,1)S(1)} copy(bf16[512,40]{0,1:T(8,128)(2,1)} %param.10) | data formatting | bytes 81920 | tf_op args[0]
  0.9 1.1 %copy.12.cx_ref = bf16[1024,40]{1,0:T(8,128)(2,1)S(1)} copy(bf16[1024,40]{0,1:T(8,128)(2,1)} %param.12) | data formatting | bytes 163840 | tf_op args[2]
  2.0 1.1 %copy.13.probes_ref = f32[1024,64]{1,0:T(8,128)S(1)} copy(f32[1024,64]{0,1:T(8,128)} %param.19) | data formatting | bytes 524288 | tf_op args[9]
  3.1 0.0 copy-start
  3.1 1.2 %copy-done = bf16[2048,256]{1,0:T(8,128)(2,1)S(1)} copy-done((bf16[2048,256]{1,0:T(8,128)(2,1)S(1)}, bf16[2048,256]{1,0:T(8,128)(2,1)}, u32[]{:S(2)}) %copy-start) | copy-done | bytes 1048600
  4.4 0.0 copy-start.1
  4.4 0.9 %copy-done.1 = bf16[40,2048]{1,0:T(8,128)(2,1)S(1)} copy-done((bf16[40,2048]{1,0:T(8,128)(2,1)S(1)}, bf16[40,2048]{1,0:T(8,128)(2,1)}, u32[]{:S(2)}) %copy-start.1) | copy-done | bytes 163864
  5.3 0.0 copy-start.2
  5.3 0.7 %copy-done.2 = f32[2048]{0:T(1024)S(1)} copy-done((f32[2048]{0:T(1024)S(1)}, f32[2048]{0:T(1024)}, u32[]{:S(2)}) %copy-start.2) | copy-done | bytes 8216
  6.0 0.0 copy-start.3
  6.0 0.7 %copy-done.3 = f32[2048]{0:T(1024)S(1)} copy-done((f32[2048]{0:T(1024)S(1)}, f32[2048]{0:T(1024)}, u32[]{:S(2)}) %copy-start.3) | copy-done | bytes 8216
  6.7 0.0 copy-start.4
  6.7 0.7 %copy-done.4 = s32[512]{0:T(512)S(1)} copy-done((s32[512]{0:T(512)S(1)}, s32[512]{0:T(512)}, u32[]{:S(2)}) %copy-start.4) | copy-done | bytes 2072
  7.3 0.0 copy-start.5
  7.3 0.7 %copy-done.5 = f32[256]{0:T(256)S(1)} copy-done((f32[256]{0:T(256)S(1)}, f32[256]{0:T(256)}, u32[]{:S(2)}) %copy-start.5) | copy-done | bytes 1048
  8.0 53.4 %shard_map.100 = f32[512,64]{1,0:T(8,128)S(1)} custom-call(bf16[512,40]{1,0:T(8,128)(2,1)S(1)} %copy.11.x_ref, s32[1,512]{1,0:T(1,128)S(1)} %bitcast.6, bf16[1024,40]{1,0:T(8,128)(2,1)S(1)} %copy.12.cx_ref, bf16[40,2048]{1,0:T(8,128)(2,1)S(1)} %copy-done.1, f32[1,2048]{1,0:T(1,128)S(1)} %bitcast.4, bf16[2048,2048]{1,0:T(8,128)(2,1)} %w2_hbm.1, ...), custom_call_target="tpu_custom_call" | custom-call | tf_op jit(solution)/shard_map/pallas_call | solution.py:244
  61.5 0.8 %copy.14 = f32[512,64]{0,1:T(8,128)} copy(f32[512,64]{1,0:T(8,128)S(1)} %shard_map.100) | data formatting | bytes 262144 | tf_op jit(solution)/shard_map/pallas_call | solution.py:244
Async XLA Ops:
  3.1 1.2 %copy-start = (bf16[2048,256]{1,0:T(8,128)(2,1)S(1)}, bf16[2048,256]{1,0:T(8,128)(2,1)}, u32[]{:S(2)}) copy-start(bf16[2048,256]{1,0:T(8,128)(2,1)} %w3_hbm.1) | copy-start | bytes 3145732
  4.4 0.9 %copy-start.1 = (bf16[40,2048]{1,0:T(8,128)(2,1)S(1)}, bf16[40,2048]{1,0:T(8,128)(2,1)}, u32[]{:S(2)}) copy-start(bf16[40,2048]{1,0:T(8,128)(2,1)} %w1_ref.1) | copy-start | bytes 491524
  5.3 0.7 %copy-start.2 = (f32[2048]{0:T(1024)S(1)}, f32[2048]{0:T(1024)}, u32[]{:S(2)}) copy-start(f32[2048]{0:T(1024)} %param.14) | copy-start | bytes 24580
  6.0 0.7 %copy-start.3 = (f32[2048]{0:T(1024)S(1)}, f32[2048]{0:T(1024)}, u32[]{:S(2)}) copy-start(f32[2048]{0:T(1024)} %param.16) | copy-start | bytes 24580
  6.7 0.7 %copy-start.4 = (s32[512]{0:T(512)S(1)}, s32[512]{0:T(512)}, u32[]{:S(2)}) copy-start(s32[512]{0:T(512)} %param.11) | copy-start | bytes 6148
  7.3 0.7 %copy-start.5 = (f32[256]{0:T(256)S(1)}, f32[256]{0:T(256)}, u32[]{:S(2)}) copy-start(f32[256]{0:T(256)} %param.18) | copy-start | bytes 3076

commit v2 on v1

--- a/solution.py
+++ b/solution.py
@@ -22,17 +22,17 @@
 
 def kernel(
     n_row, n_col, slot,
-    x_ref, dest_ref, cx_ref, w1_ref, b1_ref, w2_hbm, b2_ref, w3_hbm, rel_ref, probes_ref,
+    x_ref, dest_hbm, cx_ref, w1_ref, b1_hbm, w2_hbm, b2_hbm, w3_hbm, rel_hbm, probes_hbm,
     out_ref,
-    w2, w3, h1, h2, sent, got, colg, rowf, scaled, half_row, acc, part, parts_in,
-    w_sem, a_send, a_recv, c_send, c_recv, f_send, r_send, r_recv, p_send, p_recv,
+    dest_ref, b1_ref, b2_ref, rel_ref, probes_ref, w2, w3, h1, h2, sent, got, colg, rowf, scaled, half_row, acc, own, part, parts_in,
+    in_sem, w_sem, a_send, a_recv, c_send, c_recv, f_send, r_send, r_recv, p_send, p_recv,
 ):
     n_dev = n_row * n_col
-    rows, width = x_ref.shape
+    width, rows = x_ref.shape
     hid = w1_ref.shape[1]
     feat = w3.shape[1]
-    npr = probes_ref.shape[1]
-    cols = cx_ref.shape[0] // n_row
+    npr = probes_ref.shape[0]
+    cols = cx_ref.shape[1] // n_row
     step = hid // CHUNKS
     slots = n_dev * slot
     mr, mc = lax.axis_index("row"), lax.axis_index("col")
@@ -45,7 +45,14 @@
         for n in range(CHUNKS)
     ]
     w_copies.append(pltpu.make_async_copy(w3_hbm, w3, w_sem.at[CHUNKS]))
-    for one in w_copies:
+    pairs = (
+        (dest_hbm, dest_ref), (b1_hbm, b1_ref), (b2_hbm, b2_ref), (rel_hbm, rel_ref),
+        (probes_hbm, probes_ref),
+    )
+    in_copies = [
+        pltpu.make_async_copy(src, dst, in_sem.at[n]) for n, (src, dst) in enumerate(pairs)
+    ]
+    for one in in_copies + w_copies:
         one.start()
 
     barrier = pltpu.get_barrier_semaphore()
@@ -57,6 +64,7 @@
             barrier, inc=1, device_id=(to // n_col, to % n_col), device_id_type=MESH
         )
 
+    in_copies[0].wait()
     bits = rows.bit_length() - 1
     dest = dest_ref[...]
     target = lax.shift_right_logical(dest, jnp.full_like(dest, bits))
@@ -75,7 +83,7 @@
     line = lax.broadcasted_iota(jnp.int32, (128, rows), 0)
     marks = jnp.where(line == width, high, jnp.where(line == width + 1, low, 0.0)).astype(BF)
     sent[...] = mm(pick, marks, NT).astype(BF).reshape(n_dev, slot, 128)
-    sent[:, :, :width] = mm(pick, x_ref[...]).astype(BF).reshape(n_dev, slot, width)
+    sent[:, :, :width] = mm(pick, x_ref[...], NT).astype(BF).reshape(n_dev, slot, width)
     got[me] = sent[me]
 
     pl.semaphore_wait(barrier, n_dev - 1)
@@ -91,10 +99,10 @@
     def _(off):
         a2a((me + off) % n_dev, me).start()
 
-    def layers(x, m, first, between=None):
+    def layers(x, m, first, dims):
         for n in range(CHUNKS):
             at = pl.ds(n * step, step)
-            h1[:m, at] = jnp.maximum(mm(x, w1_ref[:, at]) + b1_ref[:, at], 0.0).astype(BF)
+            h1[:m, at] = jnp.maximum(mm(x, w1_ref[:, at], dims) + b1_ref[:, at], 0.0).astype(BF)
         if first:
             for one in w_copies[:CHUNKS]:
                 one.wait()
@@ -106,19 +114,15 @@
 
         if first:
             w_copies[CHUNKS].wait()
-        if between is not None:
-            between()
         return mm(h2[:m, :], w3[...]).astype(BF)
 
     mine = pl.ds(pl.multiple_of(mr * cols, cols), cols)
+    for one in in_copies[1:]:
+        one.wait()
     rel = rel_ref[...]
-    cf = layers(cx_ref[mine, :], cols, True)
+    cf = layers(cx_ref[:, mine], cols, True, TN)
     colg[mc, :cols, :] = cf
-    eye = (
-        lax.broadcasted_iota(jnp.int32, (cols, cols), 0)
-        == lax.broadcasted_iota(jnp.int32, (cols, cols), 1)
-    ).astype(F32).astype(BF)
-    colg[mc, pl.ds(cols, npr), :] = mm(probes_ref[mine, :].astype(BF), eye, TN).astype(BF)
+    colg[mc, pl.ds(cols, npr), :] = probes_ref[:, mine].astype(BF)
     cf32 = cf.astype(F32)
     half_col = lax.dot_general(
         jnp.broadcast_to(0.5 * rel, (16, feat)), cf32 * cf32, NT,
@@ -161,12 +165,7 @@
 
     forwards = [col_copy(mate(k), sibling, f_send.at[k]) for k in range(1, n_chip)]
 
-    def forward():
-        for k in range(1, n_chip):
-            col_copy(mate(k), sibling, f_send.at[k]).wait_recv()
-            forwards[k - 1].start()
-
-    rowf[mr] = layers(xp[:, :width], rows, False, forward)
+    rowf[mr] = layers(xp[:, :width], rows, False, NN)
 
     def row_copy(block, to, send):
         return pltpu.make_async_remote_copy(
@@ -178,6 +177,10 @@
     row_sends = [row_copy(mr, (mr + n_row - k) % n_row, r_send.at[k]) for k in range(1, n_row)]
     for one in row_sends:
         one.start()
+
+    for k in range(1, n_chip):
+        col_copy(mate(k), sibling, f_send.at[k]).wait_recv()
+        forwards[k - 1].start()
 
     for k in range(n_chip):
         other = ((chip + k) % n_chip) * 2 + 1 - core
@@ -196,7 +199,7 @@
         )
         acc[...] = jnp.zeros_like(acc)
 
-        @pl.loop(0, n_col)
+        @pl.loop(0, n_col, unroll=2)
         def _(c):
             cross = mm(scaled[...], colg[c, :cols, :], NT)
             sq = colg[c, pl.ds(cols + npr, 16), :].astype(F32)
@@ -214,15 +217,16 @@
             one.start()
             part_sends.append(one)
         else:
-            out_ref[...] = acc[...]
+            own[...] = acc[...]
 
     for k in range(n_row - 1):
         part_sends[k].wait_recv()
     total = parts_in[0].astype(F32)
     for k in range(1, n_row - 1):
         total += parts_in[k].astype(F32)
-    out_ref[:half, :] += total[:, :npr]
-    out_ref[half:, :] += total[:, npr:]
+    own[:half, :] += total[:, :npr]
+    own[half:, :] += total[:, npr:]
+    out_ref[...] = own[...].T
 
     @pl.loop(1, n_dev)
     def _(off):
@@ -239,14 +243,19 @@
     slot = -(-(rows // n_dev) // 16) * 16
     tall = max(rows, cols)
     vmem = pl.BlockSpec(memory_space=pltpu.VMEM)
-    hbm = pl.BlockSpec(memory_space=pl.ANY)
+    hbm = pl.BlockSpec(memory_space=pltpu.HBM)
     dma = pltpu.SemaphoreType.DMA
     return pl.pallas_call(
         functools.partial(kernel, n_row, n_col, slot),
-        out_shape=jax.ShapeDtypeStruct((rows, npr), F32),
-        in_specs=[vmem] * 5 + [hbm, vmem, hbm, vmem, vmem],
+        out_shape=jax.ShapeDtypeStruct((npr, rows), F32),
+        in_specs=[vmem, hbm, vmem, vmem] + [hbm] * 6,
         out_specs=vmem,
         scratch_shapes=[
+            pltpu.VMEM((1, rows), jnp.int32),
+            pltpu.VMEM((1, hid), F32),
+            pltpu.VMEM((1, hid), F32),
+            pltpu.VMEM((1, feat), F32),
+            pltpu.VMEM((npr, cols * n_row), F32),
             pltpu.VMEM((CHUNKS, hid, hid // CHUNKS), BF),
             pltpu.VMEM((hid, feat), BF),
             pltpu.VMEM((tall, hid), BF),
@@ -258,8 +267,10 @@
             pltpu.VMEM((rows, feat), BF),
             pltpu.VMEM((rows, cols), F32),
             pltpu.VMEM((rows, npr), F32),
+            pltpu.VMEM((rows, npr), F32),
             pltpu.VMEM((n_row - 1, rows // 2, 2 * npr), BF),
             pltpu.VMEM((n_row - 1, rows // 2, 2 * npr), BF),
+            dma((5,)),
             dma((CHUNKS + 1,)),
             dma((n_dev,)),
             dma((n_dev,)),
@@ -272,10 +283,10 @@
             dma((n_row,)),
         ],
         compiler_params=pltpu.CompilerParams(
-            collective_id=0, has_side_effects=True, vmem_limit_bytes=48 * 2**20
+            collective_id=0, has_side_effects=True, vmem_limit_bytes=60 * 2**20
         ),
-    )(x, dest.reshape(1, -1), cx, w1, b1.reshape(1, -1), w2, b2.reshape(1, -1), w3,
-      rel.reshape(1, -1), probes)
+    )(x.T, dest.reshape(1, -1), cx.T, w1, b1.reshape(1, -1), w2, b2.reshape(1, -1), w3,
+      rel.reshape(1, -1), probes.T).T
 
 
 def solution(mesh):

time: 62.7 us -> 49 us (0.78)
  local copies, waits for them, and re-layouts: 8.77 us -> 1.57 us
  Pallas kernels: 53.4 us -> 47.3 us
    unnamed x15 -> x1, local copies, waits for them, and re-layouts: 7.99 us -> 1.57 us
    pallas_call x1, Pallas kernels: 53.4 us -> 47.3 us  [per_device(): pl.pallas_call(functools.partial(kernel, n_row, n_col, slot), out_shape=j...]
    pallas_call x1 -> x0, local copies, waits for them, and re-layouts: 0.77 us -> none  [per_device(): pl.pallas_call(functools.partial(kernel, n_row, n_col, slot), out_shape=j...]
where the time goes in v2:
time: 49 us; the launch traced here: 48.8 us
  Pallas kernels  47.3 us (97%)
  local copies, waits for them, and re-layouts  1.57 us (3%)
    pallas_call x1, Pallas kernels, per_device(): pl.pallas_call(functools.partial(kernel, n_row, n_col, slot), out_shape=j...  47.3 us
    unnamed x1, local copies, waits for them, and re-layouts  1.57 us

profile of v2, /device:TPU:0, one launch (start us, length us, event | category | flops | bytes accessed | tf_op | source)
XLA Modules:
  0.0 48.8 jit_solution(11234358323064139023)
XLA Ops:
  0.0 47.3 %shard_map.100 = f32[64,512]{1,0:T(8,128)} custom-call(bf16[40,512]{1,0:T(8,128)(2,1)} %bitcast.11, s32[1,512]{1,0:T(1,128)} %bitcast.14, bf16[40,1024]{1,0:T(8,128)(2,1)} %bitcast.10, bf16[40,2048]{1,0:T(8,128)(2,1)} %w1_ref.1, f32[1,2048]{1,0:T(1,128)} %bitcast.12, bf16[2048,2048]{1,0:T(8,128)(2,1)} %w2_hbm.1, f32[1,2048]{1,0:T(1,128)} %bitcast.13, ...), custom_call_target="tpu_custom_call" | custom-call | tf_op jit(solution)/shard_map/pallas_call | solution.py:248
  47.3 1.6 %copy.12 = f32[512,64]{0,1:T(8,128)} copy(f32[512,64]{0,1:T(8,128)} %bitcast.8) | data formatting | bytes 262144
